TPU v7x, 256 devices: a whole 4x4x8 slice. The times are simulated.
256 devices in a mesh: prow: 16 (over y_lo, z), pcol: 16 (over x, y_hi, core).
Axes of the slice: x: 4, y: 4 (y_hi: 2, y_lo: 2; y = y_hi * 2 + y_lo), z: 8, core: 2. Of those that a mesh axis runs over, the one named last changes fastest.
Arguments:
- ancestor_inverse: bfloat16 [12288, 12288], P('pcol', 'prow'), may hold values from -0.0546875 to 0.0546875
- factor_panel: bfloat16 [3, 12288, 1024], P(None, 'prow', 'pcol'), may hold values from -1.5 to 1.5
- pattern: int32 [3, 96], replicated, may hold values 0 or 1
- diagonal_inverse: float32 [3, 1024, 1024], P(None, 'pcol', 'prow'), may hold values from -6 to 6
Outputs:
- offdiag_inverse: float32 [3, 12288, 1024], P(None, 'pcol', 'prow')
- diagonal_block: float32 [3, 1024, 1024], P(None, 'pcol', 'prow')
All inputs are finite; a program needn't handle non-finite values.
Results may differ from a plain program's by a relative error of at most 0.0003.
Values may be sent and summed in bfloat16 or wider, within the bound.
No kernel may reach another device: no remote copies, remote signals or barrier semaphores. Data moves between devices by JAX's collectives and lax.ppermute only.
A program may use at most 128 MiB of HBM per device.

v0:
```python
import jax
import jax.numpy as jnp
from jax import lax
from jax.sharding import PartitionSpec as P

BLK = 128


def spread_2(value, axis, source):
    kept = jnp.where(lax.axis_index(axis) == source, value, 0).astype(value.dtype)
    return lax.psum(kept, axis)


def local_mask(pattern, first, count, block):
    picked = lax.dynamic_slice_in_dim(pattern, first, count, 1)
    spread = jnp.broadcast_to(picked[:, :, None], (picked.shape[0], count, block))
    return spread.reshape(picked.shape[0], count * block)


def selected_step(ancestor_inverse, masked, mask_cols, diag_term):
    row_panel = lax.all_gather(masked, "pcol", axis=2, tiled=True)
    partial_value = jnp.einsum(
        "ij,kjn->kin", ancestor_inverse, row_panel, preferred_element_type=jnp.float32
    )
    group_ratio = lax.axis_size("prow") // lax.axis_size("pcol")
    col_index = lax.axis_index("pcol")
    pieces = spread_2(row_panel, "prow", col_index * group_ratio + 0)
    col_panel = pieces.astype(jnp.float32)
    reduced = lax.psum_scatter(partial_value, "prow", scatter_dimension=2, tiled=True)
    offdiag = -(reduced * mask_cols[:, :, None])
    square = jnp.einsum("kin,kim->knm", col_panel, offdiag, precision=lax.Precision.HIGHEST)
    diagonal = diag_term - lax.psum_scatter(square, "pcol", scatter_dimension=1, tiled=True)
    return (offdiag, diagonal)


def shards(ancestor_inverse, factor_panel, pattern, diagonal_inverse):
    per_prow = factor_panel.shape[1] // BLK
    per_pcol = ancestor_inverse.shape[0] // BLK
    mask_rows = local_mask(pattern, lax.axis_index("prow") * per_prow, per_prow, BLK).astype(
        jnp.bfloat16
    )
    mask_cols = local_mask(pattern, lax.axis_index("pcol") * per_pcol, per_pcol, BLK).astype(
        jnp.float32
    )
    masked = factor_panel * mask_rows[:, :, None]
    offdiag, diagonal = selected_step(ancestor_inverse, masked, mask_cols, diagonal_inverse)
    return (offdiag, diagonal)


def solution(mesh):
    in_specs = (P("pcol", "prow"), P(None, "prow", "pcol"), P(), P(None, "pcol", "prow"))
    out_specs = (P(None, "pcol", "prow"), P(None, "pcol", "prow"))
    return jax.shard_map(shards, mesh=mesh, in_specs=in_specs, out_specs=out_specs, check_vma=False)
```

profile of v0, /device:TPU:2, one launch (start us, length us, event | category | flops | bytes accessed | tf_op | source)
XLA Modules:
  0.0 442.0 jit_solution(10268001574837307801)
XLA Ops:
  7.2 0.0 copy-start
  7.2 0.0 all-gather.2.cloned.1.call-start
  7.2 0.9 dynamic-slice_convert_fusion
  8.1 0.1 broadcast_bitcast_fusion.1
  8.2 1.7 broadcast_multiply_fusion
  9.9 0.0 all-gather.2.cloned.1.call-update
  9.9 0.0 reduce-scatter.3.cloned.1.call-start
  10.0 67.2 %all-gather.2.cloned.1.call-done = bf16[3,768,1024]{1,2,0:T(8,128)(2,1)} async-done(((bf16[3,768,64]{1,2,0:T(8,128)(2,1)}), bf16[3,768,1024]{1,2,0:T(8,128)(2,1)}) %all-gather.2.cloned.1.call-update) | async-done | bytes 4718608 | tf_op jit(solution)/shard_map/all_gather | solution.py:21
  77.1 0.0 copy-done
  77.1 8.8 %convolution_bitcast_fusion = f32[3,768,1024]{1,2,0:T(8,128)} fusion(bf16[3,768,1024]{1,2,0:T(8,128)(2,1)} %all-gather.2.cloned.1.call-done, bf16[768,768]{1,0:T(8,128)(2,1)S(1)} %copy-done), kind=kOutput, calls=%fused_computation.1 | convolution fusion | flops 3623878656 | bytes 15335424 | tf_op jit(solution)/shard_map/ij,kjn->kin/dot_general | solution.py:22
  85.9 0.0 reduce-scatter.3.cloned.1.call-update
  85.9 0.0 all-reduce.2.cloned.1.call-start
  86.0 2.4 broadcast_select_fusion
  88.4 0.0 all-reduce.2.cloned.1.call-update
  88.4 0.0 reduce-scatter.5.cloned.1.call-start
  88.5 0.1 broadcast_bitcast_fusion
  88.6 108.3 %reduce-scatter.3.cloned.1.call-done = f32[3,768,64]{1,2,0:T(8,128)} async-done(((f32[3,768,1024]{1,2,0:T(8,128)}), f32[3,768,64]{1,2,0:T(8,128)}) %reduce-scatter.3.cloned.1.call-update) | async-done | bytes 589840 | tf_op jit(solution)/shard_map/reduce_scatter | solution.py:29
  196.9 0.0 copy-start.2
  196.9 1.1 multiply_negate_fusion
  198.1 0.0 copy-start.1
  198.1 155.0 %all-reduce.2.cloned.1.call-done = bf16[3,768,1024]{1,2,0:T(8,128)(2,1)} async-done(((bf16[3,768,1024]{1,2,0:T(8,128)(2,1)}), bf16[3,768,1024]{1,2,0:T(8,128)(2,1)}) %all-reduce.2.cloned.1.call-update) | async-done | bytes 4718608 | tf_op jit(solution)/shard_map/psum | solution.py:11
  353.1 7.3 %fusion.1 = f32[3,1024,64]{2,1,0:T(8,128)} fusion(bf16[3,768,1024]{1,2,0:T(8,128)(2,1)} %all-reduce.2.cloned.1.call-done, f32[3,768,64]{1,2,0:T(8,128)S(1)} %multiply_negate_fusion), kind=kOutput, calls=%fused_computation.11 | convolution fusion | flops 1811939328 | bytes 6094848 | tf_op jit(solution)/shard_map/kin,kim->knm/dot_general | solution.py:31
  360.4 0.0 reduce-scatter.5.cloned.1.call-update
  360.4 73.5 %reduce-scatter.5.cloned.1.call-done = f32[3,64,64]{2,1,0:T(8,128)} async-done(((f32[3,1024,64]{2,1,0:T(8,128)}), f32[3,64,64]{2,1,0:T(8,128)}) %reduce-scatter.5.cloned.1.call-update) | async-done | bytes 49168 | tf_op jit(solution)/shard_map/reduce_scatter | solution.py:32
  433.9 0.0 copy-done.2
  433.9 1.5 sub.3
  435.5 0.0 copy-done.1
  (2 shorter events, 0.0 us)
Async XLA Ops:
  7.2 70.0 %copy-start = (bf16[768,768]{1,0:T(8,128)(2,1)S(1)}, bf16[768,768]{1,0:T(8,128)(2,1)}, u32[]{:S(2)}) copy-start(bf16[768,768]{1,0:T(8,128)(2,1)} %param.4) | copy-start | bytes 3538948
  7.2 70.0 %all-gather.2.cloned.1.call-start = ((), (), s32[]{:S(2)}) async-start(), calls=%async_computation.2 | async-start | bytes 5013504 | tf_op jit(solution)/shard_map/all_gather | solution.py:21
  9.9 187.0 %reduce-scatter.3.cloned.1.call-start = ((), (), s32[]{:S(2)}) async-start(), calls=%async_computation.3 | async-start | bytes 10027008 | tf_op jit(solution)/shard_map/reduce_scatter | solution.py:29
  85.9 267.2 %all-reduce.2.cloned.1.call-start = ((), (), s32[]{:S(2)}) async-start(), calls=%async_computation.4 | async-start | bytes 9437184 | tf_op jit(solution)/shard_map/psum | solution.py:11
  88.4 345.5 %reduce-scatter.5.cloned.1.call-start = ((), (), s32[]{:S(2)}) async-start(), calls=%async_computation.5 | async-start | bytes 1671168 | tf_op jit(solution)/shard_map/reduce_scatter | solution.py:32
  196.9 237.0 %copy-start.2 = (f32[3,64,64]{2,1,0:T(8,128)S(1)}, f32[3,64,64]{2,1,0:T(8,128)}, u32[]{:S(2)}) copy-start(f32[3,64,64]{2,1,0:T(8,128)} %param.7) | copy-start | bytes 147460
  198.1 237.4 %copy-start.1 = (f32[3,768,64]{1,2,0:T(8,128)}, f32[3,768,64]{1,2,0:T(8,128)S(1)}, u32[]{:S(2)}) copy-start(f32[3,768,64]{1,2,0:T(8,128)S(1)} %multiply_negate_fusion) | copy-start | bytes 1769476
Sparse Core Ops, SparseCore 0:
  11.4 65.7 all-gather.1
  86.0 110.8 reduce-scatter.2
  199.6 153.4 all-reduce.1
  360.5 73.3 reduce-scatter.4
where the time goes:
time: 442 us
  waiting for transfers between devices  404 us (91%)
  matrix products  16.1 us (4%)
  between operations  13.8 us (3%)
  other arithmetic  7.69 us (2%)
    psum x1, waiting for transfers between devices, spread_2(): return lax.psum(kept, axis)  155 us
    reduce_scatter x1, waiting for transfers between devices, selected_step(): lax.psum_scatter(partial_value, 'prow', scatter_dimension=2, tiled=True)  108 us
    reduce_scatter x1, waiting for transfers between devices, selected_step(): lax.psum_scatter(square, 'pcol', scatter_dimension=1, tiled=True)  73.5 us
    all_gather x1, waiting for transfers between devices, selected_step(): row_panel = lax.all_gather(masked, 'pcol', axis=2, tiled=True)  67.2 us
  transfers between devices with their start and end apart: 4, of which 4 were waited for; matrix products, arithmetic and copies ran while one was open for 1% of the time, Pallas kernels for 0%

commit v1 on v0

--- a/solution.py
+++ b/solution.py
@@ -8,7 +8,7 @@
 
 def spread_2(value, axis, source):
     kept = jnp.where(lax.axis_index(axis) == source, value, 0).astype(value.dtype)
-    return lax.psum(kept, axis)
+    return jnp.sum(lax.all_gather(kept, axis), axis=0)
 
 
 def local_mask(pattern, first, count, block):

time: 442 us -> 1090 us (2.47)
  waiting for transfers between devices: 404 us -> 1020 us
  other arithmetic: 7.69 us -> 34.3 us
    all_gather x0 -> x1, waiting for transfers between devices: none -> 774 us  [spread_2(): return jnp.sum(lax.all_gather(kept, axis), axis=0)]
    psum x1 -> x0, waiting for transfers between devices: 155 us -> none  [spread_2(): return lax.psum(kept, axis)]
    reduce_sum x0 -> x1, other arithmetic: none -> 26.6 us  [spread_2(): return jnp.sum(lax.all_gather(kept, axis), axis=0)]
where the time goes in v1:
time: 1090 us
  waiting for transfers between devices  1020 us (94%)
  other arithmetic  34.3 us (3%)
  matrix products  16.6 us (2%)
  between operations  13.8 us (1%)
    all_gather x1, waiting for transfers between devices, spread_2(): return jnp.sum(lax.all_gather(kept, axis), axis=0)  774 us
    reduce_scatter x1, waiting for transfers between devices, selected_step(): lax.psum_scatter(partial_value, 'prow', scatter_dimension=2, tiled=True)  102 us
    reduce_scatter x1, waiting for transfers between devices, selected_step(): lax.psum_scatter(square, 'pcol', scatter_dimension=1, tiled=True)  74 us
    all_gather x1, waiting for transfers between devices, selected_step(): row_panel = lax.all_gather(masked, 'pcol', axis=2, tiled=True)  67.2 us
    reduce_sum x1, other arithmetic, spread_2(): return jnp.sum(lax.all_gather(kept, axis), axis=0)  26.6 us
  transfers between devices with their start and end apart: 4, of which 4 were waited for; matrix products, arithmetic and copies ran while one was open for 1% of the time, Pallas kernels for 0%

profile of v1, /device:TPU:2, one launch (start us, length us, event | category | flops | bytes accessed | tf_op | source)
XLA Modules:
  0.0 1088.1 jit_solution(16596551547738697070)
XLA Ops:
  7.2 0.0 copy-start
  7.2 0.0 all-gather.4.cloned.1.call-start
  7.2 0.9 dynamic-slice_convert_fusion
  8.1 0.1 broadcast_bitcast_fusion.1
  8.2 1.7 broadcast_multiply_fusion
  9.9 0.0 all-gather.4.cloned.1.call-update
  9.9 0.0 reduce-scatter.3.cloned.1.call-start
  10.0 67.2 %all-gather.4.cloned.1.call-done = bf16[3,768,1024]{1,2,0:T(8,128)(2,1)} async-done(((bf16[3,768,64]{1,2,0:T(8,128)(2,1)}), bf16[3,768,1024]{1,2,0:T(8,128)(2,1)}) %all-gather.4.cloned.1.call-update) | async-done | bytes 4718608 | tf_op jit(solution)/shard_map/all_gather | solution.py:21
  77.1 0.0 copy-done
  77.1 8.7 convolution_bitcast_fusion
  85.9 0.0 reduce-scatter.3.cloned.1.call-update
  85.9 0.0 all-gather.6.cloned.1.call-start
  86.0 2.5 broadcast_select_fusion
  88.4 6.6 copy.7
  95.1 0.0 all-gather.6.cloned.1.call-update
  95.1 0.0 reduce-scatter.5.cloned.1.call-start
  95.1 0.1 broadcast_bitcast_fusion
  95.2 101.7 %reduce-scatter.3.cloned.1.call-done = f32[3,768,64]{1,2,0:T(8,128)} async-done(((f32[3,768,1024]{1,2,0:T(8,128)}), f32[3,768,64]{1,2,0:T(8,128)}) %reduce-scatter.3.cloned.1.call-update) | async-done | bytes 589840 | tf_op jit(solution)/shard_map/reduce_scatter | solution.py:29
  196.9 1.1 multiply_negate_fusion
  198.0 0.0 copy-start.1
  198.0 773.5 %all-gather.6.cloned.1.call-done = bf16[48,768,1024]{2,1,0:T(8,128)(2,1)} async-done(((bf16[3,768,1024]{2,1,0:T(8,128)(2,1)}), bf16[48,768,1024]{2,1,0:T(8,128)(2,1)}) %all-gather.6.cloned.1.call-update) | async-done | bytes 75497488 | tf_op jit(solution)/shard_map/all_gather | solution.py:11
  971.5 26.6 %reduce_sum.12 = bf16[3,768,1024]{2,1,0:T(8,128)(2,1)} reduce(bf16[16,3,768,1024]{3,2,1,0:T(8,128)(2,1)} %bitcast.2, bf16[]{:T(256)} %constant.16.clone.1), dimensions={0}, to_apply=%region_1.2 | reduce | flops 35389440 | bytes 80216064 | tf_op jit(solution)/shard_map/reduce_sum | solution.py:11
  998.1 0.0 copy-done.1
  998.1 0.0 copy-start.2
  998.1 7.8 fusion.1
  1005.9 0.0 reduce-scatter.5.cloned.1.call-update
  1006.0 74.0 %reduce-scatter.5.cloned.1.call-done = f32[3,64,64]{2,1,0:T(8,128)} async-done(((f32[3,1024,64]{2,1,0:T(8,128)}), f32[3,64,64]{2,1,0:T(8,128)}) %reduce-scatter.5.cloned.1.call-update) | async-done | bytes 49168 | tf_op jit(solution)/shard_map/reduce_scatter | solution.py:32
  1080.0 0.0 copy-done.2
  1080.0 1.5 sub.3
  (2 shorter events, 0.0 us)
Async XLA Ops:
  7.2 70.0 %copy-start = (bf16[768,768]{1,0:T(8,128)(2,1)S(1)}, bf16[768,768]{1,0:T(8,128)(2,1)}, u32[]{:S(2)}) copy-start(bf16[768,768]{1,0:T(8,128)(2,1)} %param.4) | copy-start | bytes 3538948
  7.2 70.0 %all-gather.4.cloned.1.call-start = ((), (), s32[]{:S(2)}) async-start(), calls=%async_computation.2 | async-start | bytes 5013504 | tf_op jit(solution)/shard_map/all_gather | solution.py:21
  9.9 187.0 %reduce-scatter.3.cloned.1.call-start = ((), (), s32[]{:S(2)}) async-start(), calls=%async_computation.3 | async-start | bytes 10027008 | tf_op jit(solution)/shard_map/reduce_scatter | solution.py:29
  85.9 885.6 %all-gather.6.cloned.1.call-start = ((), (), s32[]{:S(2)}) async-start(), calls=%async_computation.5 | async-start | bytes 80216064 | tf_op jit(solution)/shard_map/all_gather | solution.py:11
  95.1 984.9 %reduce-scatter.5.cloned.1.call-start = ((), (), s32[]{:S(2)}) async-start(), calls=%async_computation.4 | async-start | bytes 1671168 | tf_op jit(solution)/shard_map/reduce_scatter | solution.py:32
  198.0 800.1 %copy-start.1 = (f32[3,768,64]{1,2,0:T(8,128)}, f32[3,768,64]{1,2,0:T(8,128)S(1)}, u32[]{:S(2)}) copy-start(f32[3,768,64]{1,2,0:T(8,128)S(1)} %multiply_negate_fusion) | copy-start | bytes 1769476
  998.1 81.9 %copy-start.2 = (f32[3,64,64]{2,1,0:T(8,128)S(1)}, f32[3,64,64]{2,1,0:T(8,128)}, u32[]{:S(2)}) copy-start(f32[3,64,64]{2,1,0:T(8,128)} %param.7) | copy-start | bytes 147460
Sparse Core Ops, SparseCore 0:
  11.4 65.7 all-gather.3
  86.0 110.8 reduce-scatter.2
  198.7 772.7 all-gather.5
  1006.1 73.8 reduce-scatter.4

commit v2 on v0

--- a/solution.py
+++ b/solution.py
@@ -18,7 +18,9 @@
 
 
 def selected_step(ancestor_inverse, masked, mask_cols, diag_term):
-    row_panel = lax.all_gather(masked, "pcol", axis=2, tiled=True)
+    row_panel = jnp.concatenate(
+        lax.all_to_all(jnp.stack([masked] * lax.axis_size("pcol")), "pcol", 0, 0), axis=2
+    )
     partial_value = jnp.einsum(
         "ij,kjn->kin", ancestor_inverse, row_panel, preferred_element_type=jnp.float32
     )

time: 442 us -> 439 us (level)
  waiting for transfers between devices: 404 us -> 336 us
  blocking collectives: 0 us -> 62.2 us
    all_gather x1 -> x0, waiting for transfers between devices: 67.2 us -> none  [selected_step(): row_panel = lax.all_gather(masked, 'pcol', axis=2, tiled=True)]
    all_to_all x0 -> x1, blocking collectives: none -> 62.2 us  [selected_step(): lax.all_to_all(jnp.stack([masked] * lax.axis_size('pcol')), 'pcol', 0, 0)]
  transfers between devices with their start and end apart: 4 -> 3, of which waited for: 4 -> 3; matrix products, arithmetic and copies ran while one was open for 1% -> 1% of each run, Pallas kernels for 0% -> 0%
where the time goes in v2:
time: 439 us
  waiting for transfers between devices  336 us (77%)
  blocking collectives  62.2 us (14%)
  between operations  13.8 us (3%)
  matrix products  13.7 us (3%)
  other arithmetic  9.3 us (2%)
    psum x1, waiting for transfers between devices, spread_2(): return lax.psum(kept, axis)  155 us
    reduce_scatter x1, waiting for transfers between devices, selected_step(): lax.psum_scatter(partial_value, 'prow', scatter_dimension=2, tiled=True)  107 us
    reduce_scatter x1, waiting for transfers between devices, selected_step(): lax.psum_scatter(square, 'pcol', scatter_dimension=1, tiled=True)  73.5 us
    all_to_all x1, blocking collectives, selected_step(): lax.all_to_all(jnp.stack([masked] * lax.axis_size('pcol')), 'pcol', 0, 0)  62.2 us
  transfers between devices with their start and end apart: 3, of which 3 were waited for; matrix products, arithmetic and copies ran while one was open for 1% of the time, Pallas kernels for 0%

profile of v2, /device:TPU:2, one launch (start us, length us, event | category | flops | bytes accessed | tf_op | source)
XLA Modules:
  0.0 438.7 jit_solution(17746654641403492135)
XLA Ops:
  7.2 0.0 copy-start
  7.2 0.0 reduce-scatter.3.cloned.1.call-start
  7.2 0.9 dynamic-slice_convert_fusion
  8.1 0.1 broadcast_bitcast_fusion.1
  8.2 1.0 broadcast_multiply_fusion
  9.2 0.6 stack.2
  9.7 62.2 %all_to_all.5 = bf16[16,3,768,64]{2,3,1,0:T(8,128)(2,1)S(1)} all-to-all(bf16[16,3,768,64]{2,3,1,0:T(8,128)(2,1)S(1)} %stack.2), channel_id=1, replica_groups=mesh['prow'=16,'pcol'=16] {'pcol'}, dimensions={0} | all-to-all | bytes 9437184 | tf_op jit(solution)/shard_map/all_to_all | solution.py:22
  71.9 0.5 copy.6
  72.5 0.0 copy-start.1
  72.5 2.2 copy-done.1
  74.7 0.0 copy-done
  74.7 6.4 %convolution_bitcast_fusion = f32[3,768,1024]{1,2,0:T(8,128)} fusion(bf16[3,768,1024]{1,2,0:T(8,128)(2,1)S(1)} %bitcast.21, bf16[768,768]{1,0:T(8,128)(2,1)S(1)} %copy-done), kind=kOutput, calls=%fused_computation.1 | convolution fusion | flops 3623878656 | bytes 15335424 | tf_op jit(solution)/shard_map/ij,kjn->kin/dot_general | solution.py:24
  81.1 0.0 reduce-scatter.3.cloned.1.call-update
  81.2 0.0 all-reduce.2.cloned.1.call-start
  81.2 4.8 %broadcast_select_fusion = bf16[3,768,1024]{1,2,0:T(8,128)(2,1)} fusion(pred[]{:T(512)S(6)} %eq.3, bf16[3,768,16,64]{1,3,2,0:T(8,128)(2,1)} %copy-done.1), kind=kLoop, calls=%fused_computation | loop fusion | flops 2359296 | bytes 9437185 | tf_op jit(solution)/shard_map/jit(_where)/select_n | solution.py:10
  86.0 0.0 all-reduce.2.cloned.1.call-update
  86.0 0.0 reduce-scatter.5.cloned.1.call-start
  86.1 0.1 broadcast_bitcast_fusion
  86.1 107.5 %reduce-scatter.3.cloned.1.call-done = f32[3,768,64]{1,2,0:T(8,128)} async-done(((f32[3,768,1024]{1,2,0:T(8,128)}), f32[3,768,64]{1,2,0:T(8,128)}) %reduce-scatter.3.cloned.1.call-update) | async-done | bytes 589840 | tf_op jit(solution)/shard_map/reduce_scatter | solution.py:31
  193.6 0.0 copy-start.3
  193.6 1.1 multiply_negate_fusion
  194.8 0.0 copy-start.2
  194.8 154.9 %all-reduce.2.cloned.1.call-done = bf16[3,768,1024]{1,2,0:T(8,128)(2,1)} async-done(((bf16[3,768,1024]{1,2,0:T(8,128)(2,1)}), bf16[3,768,1024]{1,2,0:T(8,128)(2,1)}) %all-reduce.2.cloned.1.call-update) | async-done | bytes 4718608 | tf_op jit(solution)/shard_map/psum | solution.py:11
  349.7 7.3 %fusion.1 = f32[3,1024,64]{2,1,0:T(8,128)} fusion(bf16[3,768,1024]{1,2,0:T(8,128)(2,1)} %all-reduce.2.cloned.1.call-done, f32[3,768,64]{1,2,0:T(8,128)S(1)} %multiply_negate_fusion), kind=kOutput, calls=%fused_computation.11 | convolution fusion | flops 1811939328 | bytes 6094848 | tf_op jit(solution)/shard_map/kin,kim->knm/dot_general | solution.py:33
  357.0 0.0 reduce-scatter.5.cloned.1.call-update
  357.1 73.5 %reduce-scatter.5.cloned.1.call-done = f32[3,64,64]{2,1,0:T(8,128)} async-done(((f32[3,1024,64]{2,1,0:T(8,128)}), f32[3,64,64]{2,1,0:T(8,128)}) %reduce-scatter.5.cloned.1.call-update) | async-done | bytes 49168 | tf_op jit(solution)/shard_map/reduce_scatter | solution.py:34
  430.6 0.0 copy-done.3
  430.6 1.5 sub.3
  432.1 0.0 copy-done.2
  (2 shorter events, 0.0 us)
Async XLA Ops:
  7.2 67.5 %copy-start = (bf16[768,768]{1,0:T(8,128)(2,1)S(1)}, bf16[768,768]{1,0:T(8,128)(2,1)}, u32[]{:S(2)}) copy-start(bf16[768,768]{1,0:T(8,128)(2,1)} %param.4) | copy-start | bytes 3538948
  7.2 186.4 %reduce-scatter.3.cloned.1.call-start = ((), (), s32[]{:S(2)}) async-start(), calls=%async_computation.3 | async-start | bytes 10027008 | tf_op jit(solution)/shard_map/reduce_scatter | solution.py:31
  72.5 2.2 copy-start.1
  81.2 268.6 %all-reduce.2.cloned.1.call-start = ((), (), s32[]{:S(2)}) async-start(), calls=%async_computation.4 | async-start | bytes 9437184 | tf_op jit(solution)/shard_map/psum | solution.py:11
  86.0 344.6 %reduce-scatter.5.cloned.1.call-start = ((), (), s32[]{:S(2)}) async-start(), calls=%async_computation.5 | async-start | bytes 1671168 | tf_op jit(solution)/shard_map/reduce_scatter | solution.py:34
  193.6 237.0 %copy-start.3 = (f32[3,64,64]{2,1,0:T(8,128)S(1)}, f32[3,64,64]{2,1,0:T(8,128)}, u32[]{:S(2)}) copy-start(f32[3,64,64]{2,1,0:T(8,128)} %param.7) | copy-start | bytes 147460
  194.8 237.4 %copy-start.2 = (f32[3,768,64]{1,2,0:T(8,128)}, f32[3,768,64]{1,2,0:T(8,128)S(1)}, u32[]{:S(2)}) copy-start(f32[3,768,64]{1,2,0:T(8,128)S(1)} %multiply_negate_fusion) | copy-start | bytes 1769476
Sparse Core Ops, SparseCore 0:
  81.3 112.2 reduce-scatter.2
  196.3 153.3 all-reduce.1
  357.2 73.3 reduce-scatter.4
